TPU v7x, 32 devices: a whole 2x2x4 slice. The times are simulated.
32 devices in a mesh: gx: 16 (over z, y, x), gy: 2 (over core).
Axes of the slice: x: 2, y: 2, z: 4, core: 2. Of those that a mesh axis runs over, the one named last changes fastest.
Arguments:
- noisy: bfloat16 [2, 1024, 512], P(None, 'gx', 'gy'), may hold values from -6 to 6
- dilations: int32 [3], replicated, may hold values from 1 to 256, as said below
- conv_weights: float32 [3, 4, 27], replicated, may hold values from -0.625 to 0.625
- biases: float32 [3], replicated, may hold values from -3 to 3
- mix_weights: float32 [4], replicated, may hold values from -3 to 3
Outputs:
- denoised: bfloat16 [2, 1024, 512], P(None, 'gx', 'gy')
Inputs may be any that keep to these rules, and one draw needn't show every extreme that they name: `dilations`: every layer's dilation lies in 1 .. 256; some layer has dilation 256.
All inputs are finite; a program needn't handle non-finite values.
Results may differ from a plain program's by a relative error of at most 0.0065.
Values sent between devices are 32-bit elements; how exact they have to be, the bound alone decides.
No kernel may reach another device: no remote copies, remote signals or barrier semaphores. Data moves between devices by JAX's collectives and lax.ppermute only.
A program may use at most 64 MiB of HBM per device.

v0:
```python
import jax
import jax.numpy as jnp
from jax import lax
from jax.sharding import PartitionSpec as P

LAYERS = 3
DMAX = 256


def from_behind(value, axis, steps):
    count = lax.axis_size(axis)
    leading, last = (max(0, -steps), min(count, count - steps))
    return lax.ppermute(value, axis, [(source, source + steps) for source in range(leading, last)])


def tap_sums(feature_maps, layer_weights):
    map_count = len(feature_maps)
    stacked = jnp.stack(feature_maps)
    padded = jnp.pad(stacked, ((0, 0), (1, 1), (0, 0), (0, 0)))
    depth = stacked.shape[1]
    zstack = jnp.stack([padded[:, shift_index : shift_index + depth] for shift_index in range(3)])
    kernel = layer_weights[:map_count].reshape(map_count, 3, 3, 3)
    return jnp.einsum(
        "cjzxy,jcab->abzxy",
        zstack,
        kernel,
        precision=lax.Precision.HIGHEST,
        preferred_element_type=jnp.float32,
    )


def hops_up(source_field, steps):
    return from_behind(source_field, "gx", -steps)


def hops_down(source_field, steps):
    return from_behind(source_field, "gx", steps)


def fetch_x(stacked, reach, mover, upward):
    x_dim = stacked.ndim - 2
    width = stacked.shape[x_dim]
    tile_count = reach // width
    remainder = reach % width
    nearby = mover(stacked, 1)
    if upward:
        joined = jnp.concatenate([stacked, nearby], axis=x_dim)
        start_index = remainder
    else:
        joined = jnp.concatenate([nearby, stacked], axis=x_dim)
        start_index = width - remainder
    shifted = lax.dynamic_slice_in_dim(joined, start_index, width, x_dim)
    for level in range((DMAX // width).bit_length()):
        distant = mover(shifted, 1 << level)
        shifted = jnp.where((tile_count >> level) % 2 == 1, distant, shifted)
    return shifted


def combine_x(lower_terms, middle_terms, upper_terms, reach):
    above = fetch_x(upper_terms, reach, hops_up, True)
    below = fetch_x(lower_terms, reach, hops_down, False)
    return middle_terms + above + below


def combine_y(lower_terms, middle_terms, upper_terms, reach):
    y_dim = middle_terms.ndim - 1
    height = middle_terms.shape[y_dim]
    following = from_behind(upper_terms, "gy", -1)
    joined_up = jnp.concatenate([upper_terms, following], axis=y_dim)
    above = lax.dynamic_slice_in_dim(joined_up, reach, height, y_dim)
    previous = from_behind(lower_terms, "gy", 1)
    joined_down = jnp.concatenate([previous, lower_terms], axis=y_dim)
    below = lax.dynamic_slice_in_dim(joined_down, height - reach, height, y_dim)
    return middle_terms + above + below


def body(noisy, dilations, conv_weights, biases, mix_weights):
    feature_maps = [noisy]
    for layer_index in range(LAYERS):
        reach = dilations[layer_index]
        partial_value = tap_sums(feature_maps, conv_weights[layer_index])
        column_sums = combine_y(
            partial_value[:, 0], partial_value[:, 1], partial_value[:, 2], reach
        )
        summed = combine_x(column_sums[0], column_sums[1], column_sums[2], reach)
        feature_maps.append(jax.nn.relu(summed + biases[layer_index]).astype(jnp.bfloat16))
    output = jnp.zeros(noisy.shape, jnp.float32)
    for map_index in range(LAYERS + 1):
        output = output + mix_weights[map_index] * feature_maps[map_index].astype(jnp.float32)
    return output.astype(jnp.bfloat16)


def solution(mesh):
    return jax.shard_map(
        body,
        mesh=mesh,
        in_specs=(P(None, "gx", "gy"), P(), P(), P(), P()),
        out_specs=P(None, "gx", "gy"),
        check_vma=False,
    )
```

profile of v0, /device:TPU:0, one launch (start us, length us, event | category | flops | bytes accessed | tf_op | source)
XLA Modules:
  0.0 151.6 jit_solution(53060130616551639)
XLA Ops:
  6.4 3.1 %collective-permute-start.1 = (f32[3,2,64,256]{3,2,1,0:T(8,128)S(1)}, f32[3,2,64,256]{3,2,1,0:T(8,128)S(1)}, u32[]{:S(2)}, u32[]{:S(2)}) collective-permute-start(f32[3,2,64,256]{3,2,1,0:T(8,128)S(1)} %bitcast.147), channel_id=1, source_target_pairs={{0,1},{2,3},{4,5},{6,7},{8,9},{10,11},{12,13},{14,15},{16,17},{18,... | collective-permute-start | bytes 1179656 | tf_op jit(solution)/shard_map/ppermute | solution.py:13
  16.7 5.6 %collective-permute-start.6 = (f32[2,64,256]{2,1,0:T(8,128)S(1)}, f32[2,64,256]{2,1,0:T(8,128)S(1)}, u32[]{:S(2)}, u32[]{:S(2)}) collective-permute-start(f32[2,64,256]{2,1,0:T(8,128)S(1)} %get-tuple-element.19), channel_id=1, source_target_pairs={{0,2},{2,4},{4,6},{6,8},{8,10},{10,12},{12,14},{14,16},{16,18},{18... | collective-permute-start | bytes 393224 | tf_op jit(solution)/shard_map/ppermute | solution.py:13
  24.4 1.6 %collective-permute-done.6 = f32[2,64,256]{2,1,0:T(8,128)S(1)} collective-permute-done((f32[2,64,256]{2,1,0:T(8,128)S(1)}, f32[2,64,256]{2,1,0:T(8,128)S(1)}, u32[]{:S(2)}, u32[]{:S(2)}) %collective-permute-start.6) | collective-permute-done | bytes 131104 | tf_op jit(solution)/shard_map/ppermute | solution.py:13
  26.0 4.9 %collective-permute-start.7 = (f32[2,64,256]{2,1,0:T(8,128)S(1)}, f32[2,64,256]{2,1,0:T(8,128)S(1)}, u32[]{:S(2)}, u32[]{:S(2)}) collective-permute-start(f32[2,64,256]{2,1,0:T(8,128)S(1)} %fusion.30), channel_id=1, source_target_pairs={{0,2},{2,4},{4,6},{6,8},{8,10},{10,12},{12,14},{14,16},{16,18},{18... | collective-permute-start | bytes 393224 | tf_op jit(solution)/shard_map/ppermute | solution.py:13
  32.3 2.4 %collective-permute-done.7 = f32[2,64,256]{2,1,0:T(8,128)S(1)} collective-permute-done((f32[2,64,256]{2,1,0:T(8,128)S(1)}, f32[2,64,256]{2,1,0:T(8,128)S(1)}, u32[]{:S(2)}, u32[]{:S(2)}) %collective-permute-start.7) | collective-permute-done | bytes 131104 | tf_op jit(solution)/shard_map/ppermute | solution.py:13
  34.7 6.4 %collective-permute-start.8 = (f32[2,64,256]{2,1,0:T(8,128)S(1)}, f32[2,64,256]{2,1,0:T(8,128)S(1)}, u32[]{:S(2)}, u32[]{:S(2)}) collective-permute-start(f32[2,64,256]{2,1,0:T(8,128)S(1)} %broadcast_select_fusion.8), channel_id=1, source_target_pairs={{0,4},{2,6},{4,8},{6,10},{8,12},{10,14},{12,16},{14,18},{16,20},{1... | collective-permute-start | bytes 393224 | tf_op jit(solution)/shard_map/ppermute | solution.py:13
  43.6 6.5 %collective-permute-start.9 = (f32[2,64,256]{2,1,0:T(8,128)S(1)}, f32[2,64,256]{2,1,0:T(8,128)S(1)}, u32[]{:S(2)}, u32[]{:S(2)}) collective-permute-start(f32[2,64,256]{2,1,0:T(8,128)S(1)} %broadcast_select_fusion.10), channel_id=1, source_target_pairs={{0,8},{2,10},{4,12},{6,14},{8,16},{10,18},{12,20},{14,22},{16,24},... | collective-permute-start | bytes 393224 | tf_op jit(solution)/shard_map/ppermute | solution.py:13
  50.9 1.7 %collective-permute-done.9 = f32[2,64,256]{2,1,0:T(8,128)S(1)} collective-permute-done((f32[2,64,256]{2,1,0:T(8,128)S(1)}, f32[2,64,256]{2,1,0:T(8,128)S(1)}, u32[]{:S(2)}, u32[]{:S(2)}) %collective-permute-start.9) | collective-permute-done | bytes 131104 | tf_op jit(solution)/shard_map/ppermute | solution.py:13
  53.9 2.1 %convolution_bitcast_fusion.1 = f32[3,3,2,64,256]{4,1,0,3,2:T(4,128)S(1)} fusion(bf16[1,2,2,64,256]{4,0,1,3,2:T(2,128)(2,1)S(1)} %copy.251, bf16[1,2,2,64,256]{4,0,1,3,2:T(2,128)(2,1)S(1)} %copy.250, bf16[1,2,2,64,256]{4,0,1,3,2:T(2,128)(2,1)S(1)} %copy.249, f32[2,3,3,3,1,1]{3,2,1,0,5,4:T(4,128)S(1)} %bitcast.159), kind=kOutput, calls=%fused_computation.1 | convolution fusion | flops 22413312 | bytes 1573080 | tf_op jit(solution)/shard_map/cjzxy,jcab->abzxy/dot_general | solution.py:23
  58.3 3.1 %collective-permute-start.11 = (f32[3,2,64,256]{3,2,1,0:T(8,128)S(1)}, f32[3,2,64,256]{3,2,1,0:T(8,128)S(1)}, u32[]{:S(2)}, u32[]{:S(2)}) collective-permute-start(f32[3,2,64,256]{3,2,1,0:T(8,128)S(1)} %bitcast.153), channel_id=1, source_target_pairs={{0,1},{2,3},{4,5},{6,7},{8,9},{10,11},{12,13},{14,15},{16,17},{18,... | collective-permute-start | bytes 1179656 | tf_op jit(solution)/shard_map/ppermute | solution.py:13
  67.0 4.6 %collective-permute-start.16 = (f32[2,64,256]{2,1,0:T(8,128)S(1)}, f32[2,64,256]{2,1,0:T(8,128)S(1)}, u32[]{:S(2)}, u32[]{:S(2)}) collective-permute-start(f32[2,64,256]{2,1,0:T(8,128)S(1)} %get-tuple-element.17), channel_id=1, source_target_pairs={{0,2},{2,4},{4,6},{6,8},{8,10},{10,12},{12,14},{14,16},{16,18},{18... | collective-permute-start | bytes 393224 | tf_op jit(solution)/shard_map/ppermute | solution.py:13
  74.1 4.4 %collective-permute-start.17 = (f32[2,64,256]{2,1,0:T(8,128)S(1)}, f32[2,64,256]{2,1,0:T(8,128)S(1)}, u32[]{:S(2)}, u32[]{:S(2)}) collective-permute-start(f32[2,64,256]{2,1,0:T(8,128)S(1)} %fusion.28), channel_id=1, source_target_pairs={{0,2},{2,4},{4,6},{6,8},{8,10},{10,12},{12,14},{14,16},{16,18},{18... | collective-permute-start | bytes 393224 | tf_op jit(solution)/shard_map/ppermute | solution.py:13
  79.8 2.2 %collective-permute-done.17 = f32[2,64,256]{2,1,0:T(8,128)S(1)} collective-permute-done((f32[2,64,256]{2,1,0:T(8,128)S(1)}, f32[2,64,256]{2,1,0:T(8,128)S(1)}, u32[]{:S(2)}, u32[]{:S(2)}) %collective-permute-start.17) | collective-permute-done | bytes 131104 | tf_op jit(solution)/shard_map/ppermute | solution.py:13
  82.1 4.5 %collective-permute-start.18 = (f32[2,64,256]{2,1,0:T(8,128)S(1)}, f32[2,64,256]{2,1,0:T(8,128)S(1)}, u32[]{:S(2)}, u32[]{:S(2)}) collective-permute-start(f32[2,64,256]{2,1,0:T(8,128)S(1)} %broadcast_select_fusion.4), channel_id=1, source_target_pairs={{0,4},{2,6},{4,8},{6,10},{8,12},{10,14},{12,16},{14,18},{16,20},{1... | collective-permute-start | bytes 393224 | tf_op jit(solution)/shard_map/ppermute | solution.py:13
  89.1 8.5 %collective-permute-start.19 = (f32[2,64,256]{2,1,0:T(8,128)S(1)}, f32[2,64,256]{2,1,0:T(8,128)S(1)}, u32[]{:S(2)}, u32[]{:S(2)}) collective-permute-start(f32[2,64,256]{2,1,0:T(8,128)S(1)} %broadcast_select_fusion.6), channel_id=1, source_target_pairs={{0,8},{2,10},{4,12},{6,14},{8,16},{10,18},{12,20},{14,22},{16,24},... | collective-permute-start | bytes 393224 | tf_op jit(solution)/shard_map/ppermute | solution.py:13
  97.9 2.0 %collective-permute-done.19 = f32[2,64,256]{2,1,0:T(8,128)S(1)} collective-permute-done((f32[2,64,256]{2,1,0:T(8,128)S(1)}, f32[2,64,256]{2,1,0:T(8,128)S(1)}, u32[]{:S(2)}, u32[]{:S(2)}) %collective-permute-start.19) | collective-permute-done | bytes 131104 | tf_op jit(solution)/shard_map/ppermute | solution.py:13
  105.6 3.1 %collective-permute-start.21 = (f32[3,2,64,256]{3,2,1,0:T(8,128)S(1)}, f32[3,2,64,256]{3,2,1,0:T(8,128)S(1)}, u32[]{:S(2)}, u32[]{:S(2)}) collective-permute-start(f32[3,2,64,256]{3,2,1,0:T(8,128)S(1)} %bitcast.151), channel_id=1, source_target_pairs={{0,1},{2,3},{4,5},{6,7},{8,9},{10,11},{12,13},{14,15},{16,17},{18,... | collective-permute-start | bytes 1179656 | tf_op jit(solution)/shard_map/ppermute | solution.py:13
  115.0 4.6 %collective-permute-start.26 = (f32[2,64,256]{2,1,0:T(8,128)S(1)}, f32[2,64,256]{2,1,0:T(8,128)S(1)}, u32[]{:S(2)}, u32[]{:S(2)}) collective-permute-start(f32[2,64,256]{2,1,0:T(8,128)S(1)} %get-tuple-element.15), channel_id=1, source_target_pairs={{0,2},{2,4},{4,6},{6,8},{8,10},{10,12},{12,14},{14,16},{16,18},{18... | collective-permute-start | bytes 393224 | tf_op jit(solution)/shard_map/ppermute | solution.py:13
  122.2 4.4 %collective-permute-start.27 = (f32[2,64,256]{2,1,0:T(8,128)S(1)}, f32[2,64,256]{2,1,0:T(8,128)S(1)}, u32[]{:S(2)}, u32[]{:S(2)}) collective-permute-start(f32[2,64,256]{2,1,0:T(8,128)S(1)} %fusion.26), channel_id=1, source_target_pairs={{0,2},{2,4},{4,6},{6,8},{8,10},{10,12},{12,14},{14,16},{16,18},{18... | collective-permute-start | bytes 393224 | tf_op jit(solution)/shard_map/ppermute | solution.py:13
  127.9 2.2 %collective-permute-done.27 = f32[2,64,256]{2,1,0:T(8,128)S(1)} collective-permute-done((f32[2,64,256]{2,1,0:T(8,128)S(1)}, f32[2,64,256]{2,1,0:T(8,128)S(1)}, u32[]{:S(2)}, u32[]{:S(2)}) %collective-permute-start.27) | collective-permute-done | bytes 131104 | tf_op jit(solution)/shard_map/ppermute | solution.py:13
  130.1 4.4 %collective-permute-start.28 = (f32[2,64,256]{2,1,0:T(8,128)S(1)}, f32[2,64,256]{2,1,0:T(8,128)S(1)}, u32[]{:S(2)}, u32[]{:S(2)}) collective-permute-start(f32[2,64,256]{2,1,0:T(8,128)S(1)} %broadcast_select_fusion), channel_id=1, source_target_pairs={{0,4},{2,6},{4,8},{6,10},{8,12},{10,14},{12,16},{14,18},{16,20},{1... | collective-permute-start | bytes 393224 | tf_op jit(solution)/shard_map/ppermute | solution.py:13
  137.0 8.4 %collective-permute-start.29 = (f32[2,64,256]{2,1,0:T(8,128)S(1)}, f32[2,64,256]{2,1,0:T(8,128)S(1)}, u32[]{:S(2)}, u32[]{:S(2)}) collective-permute-start(f32[2,64,256]{2,1,0:T(8,128)S(1)} %broadcast_select_fusion.2), channel_id=1, source_target_pairs={{0,8},{2,10},{4,12},{6,14},{8,16},{10,18},{12,20},{14,22},{16,24},... | collective-permute-start | bytes 393224 | tf_op jit(solution)/shard_map/ppermute | solution.py:13
  146.1 1.8 %collective-permute-done.29 = f32[2,64,256]{2,1,0:T(8,128)S(1)} collective-permute-done((f32[2,64,256]{2,1,0:T(8,128)S(1)}, f32[2,64,256]{2,1,0:T(8,128)S(1)}, u32[]{:S(2)}, u32[]{:S(2)}) %collective-permute-start.29) | collective-permute-done | bytes 131104 | tf_op jit(solution)/shard_map/ppermute | solution.py:13
  147.9 3.7 %add_convert_fusion = bf16[2,64,256]{2,1,0:T(8,128)(2,1)} fusion(bf16[2,64,256]{2,1,0:T(8,128)(2,1)S(1)} %fusion.43, bf16[2,64,256]{2,1,0:T(8,128)(2,1)S(1)} %fusion.48, bf16[2,64,256]{2,1,0:T(8,128)(2,1)S(1)} %copy-done, f32[2,64,256]{2,1,0:T(8,128)S(1)} %collective-permute-done.29, f32[2,64,256]{2,1,0:T(8,128)S(1)} %broadcast_select_fusion.2, ...), kind=kLoop, calls=%fused_computation.102 | loop fusion | flops 622592 | bytes 917525 | tf_op jit(solution)/shard_map/convert_element_type | solution.py:90
  (109 shorter events, 39.7 us)
Async XLA Ops:
  5.1 8.4 %collective-permute-start = (f32[3,2,64,256]{3,2,1,0:T(8,128)S(1)}, f32[3,2,64,256]{3,2,1,0:T(8,128)S(1)}, u32[]{:S(2)}, u32[]{:S(2)}) collective-permute-start(f32[3,2,64,256]{3,2,1,0:T(8,128)S(1)} %bitcast.143), channel_id=1, source_target_pairs={{1,0},{3,2},{5,4},{7,6},{9,8},{11,10},{13,12},{15,14},{17,16},{19,... | collective-permute-start | bytes 1179656 | tf_op jit(solution)/shard_map/ppermute | solution.py:13
  6.4 7.1 %collective-permute-start.1 = (f32[3,2,64,256]{3,2,1,0:T(8,128)S(1)}, f32[3,2,64,256]{3,2,1,0:T(8,128)S(1)}, u32[]{:S(2)}, u32[]{:S(2)}) collective-permute-start(f32[3,2,64,256]{3,2,1,0:T(8,128)S(1)} %bitcast.147), channel_id=1, source_target_pairs={{0,1},{2,3},{4,5},{6,7},{8,9},{10,11},{12,13},{14,15},{16,17},{18,... | collective-permute-start | bytes 1179656 | tf_op jit(solution)/shard_map/ppermute | solution.py:13
  14.0 8.3 %collective-permute-start.2 = (f32[2,64,256]{2,1,0:T(8,128)S(1)}, f32[2,64,256]{2,1,0:T(8,128)S(1)}, u32[]{:S(2)}, u32[]{:S(2)}) collective-permute-start(f32[2,64,256]{2,1,0:T(8,128)S(1)} %get-tuple-element.18), channel_id=1, source_target_pairs={{2,0},{4,2},{6,4},{8,6},{10,8},{12,10},{14,12},{16,14},{18,16},{20... | collective-permute-start | bytes 393224 | tf_op jit(solution)/shard_map/ppermute | solution.py:13
  16.7 9.3 %collective-permute-start.6 = (f32[2,64,256]{2,1,0:T(8,128)S(1)}, f32[2,64,256]{2,1,0:T(8,128)S(1)}, u32[]{:S(2)}, u32[]{:S(2)}) collective-permute-start(f32[2,64,256]{2,1,0:T(8,128)S(1)} %get-tuple-element.19), channel_id=1, source_target_pairs={{0,2},{2,4},{4,6},{6,8},{8,10},{10,12},{12,14},{14,16},{16,18},{18... | collective-permute-start | bytes 393224 | tf_op jit(solution)/shard_map/ppermute | solution.py:13
  22.4 8.6 %collective-permute-start.3 = (f32[2,64,256]{2,1,0:T(8,128)S(1)}, f32[2,64,256]{2,1,0:T(8,128)S(1)}, u32[]{:S(2)}, u32[]{:S(2)}) collective-permute-start(f32[2,64,256]{2,1,0:T(8,128)S(1)} %fusion.31), channel_id=1, source_target_pairs={{2,0},{4,2},{6,4},{8,6},{10,8},{12,10},{14,12},{16,14},{18,16},{20... | collective-permute-start | bytes 393224 | tf_op jit(solution)/shard_map/ppermute | solution.py:13
  26.0 8.6 %collective-permute-start.7 = (f32[2,64,256]{2,1,0:T(8,128)S(1)}, f32[2,64,256]{2,1,0:T(8,128)S(1)}, u32[]{:S(2)}, u32[]{:S(2)}) collective-permute-start(f32[2,64,256]{2,1,0:T(8,128)S(1)} %fusion.30), channel_id=1, source_target_pairs={{0,2},{2,4},{4,6},{6,8},{8,10},{10,12},{12,14},{14,16},{16,18},{18... | collective-permute-start | bytes 393224 | tf_op jit(solution)/shard_map/ppermute | solution.py:13
  31.0 10.1 %collective-permute-start.4 = (f32[2,64,256]{2,1,0:T(8,128)S(1)}, f32[2,64,256]{2,1,0:T(8,128)S(1)}, u32[]{:S(2)}, u32[]{:S(2)}) collective-permute-start(f32[2,64,256]{2,1,0:T(8,128)S(1)} %broadcast_select_fusion.9), channel_id=1, source_target_pairs={{4,0},{6,2},{8,4},{10,6},{12,8},{14,10},{16,12},{18,14},{20,16},{2... | collective-permute-start | bytes 393224 | tf_op jit(solution)/shard_map/ppermute | solution.py:13
  34.7 8.9 %collective-permute-start.8 = (f32[2,64,256]{2,1,0:T(8,128)S(1)}, f32[2,64,256]{2,1,0:T(8,128)S(1)}, u32[]{:S(2)}, u32[]{:S(2)}) collective-permute-start(f32[2,64,256]{2,1,0:T(8,128)S(1)} %broadcast_select_fusion.8), channel_id=1, source_target_pairs={{0,4},{2,6},{4,8},{6,10},{8,12},{10,14},{12,16},{14,18},{16,20},{1... | collective-permute-start | bytes 393224 | tf_op jit(solution)/shard_map/ppermute | solution.py:13
  41.1 9.8 %collective-permute-start.5 = (f32[2,64,256]{2,1,0:T(8,128)S(1)}, f32[2,64,256]{2,1,0:T(8,128)S(1)}, u32[]{:S(2)}, u32[]{:S(2)}) collective-permute-start(f32[2,64,256]{2,1,0:T(8,128)S(1)} %broadcast_select_fusion.11), channel_id=1, source_target_pairs={{8,0},{10,2},{12,4},{14,6},{16,8},{18,10},{20,12},{22,14},{24,16},... | collective-permute-start | bytes 393224 | tf_op jit(solution)/shard_map/ppermute | solution.py:13
  43.6 9.0 %collective-permute-start.9 = (f32[2,64,256]{2,1,0:T(8,128)S(1)}, f32[2,64,256]{2,1,0:T(8,128)S(1)}, u32[]{:S(2)}, u32[]{:S(2)}) collective-permute-start(f32[2,64,256]{2,1,0:T(8,128)S(1)} %broadcast_select_fusion.10), channel_id=1, source_target_pairs={{0,8},{2,10},{4,12},{6,14},{8,16},{10,18},{12,20},{14,22},{16,24},... | collective-permute-start | bytes 393224 | tf_op jit(solution)/shard_map/ppermute | solution.py:13
  56.9 7.2 %collective-permute-start.10 = (f32[3,2,64,256]{3,2,1,0:T(8,128)S(1)}, f32[3,2,64,256]{3,2,1,0:T(8,128)S(1)}, u32[]{:S(2)}, u32[]{:S(2)}) collective-permute-start(f32[3,2,64,256]{3,2,1,0:T(8,128)S(1)} %bitcast.149), channel_id=1, source_target_pairs={{1,0},{3,2},{5,4},{7,6},{9,8},{11,10},{13,12},{15,14},{17,16},{19,... | collective-permute-start | bytes 1179656 | tf_op jit(solution)/shard_map/ppermute | solution.py:13
  64.6 7.0 %collective-permute-start.12 = (f32[2,64,256]{2,1,0:T(8,128)S(1)}, f32[2,64,256]{2,1,0:T(8,128)S(1)}, u32[]{:S(2)}, u32[]{:S(2)}) collective-permute-start(f32[2,64,256]{2,1,0:T(8,128)S(1)} %get-tuple-element.16), channel_id=1, source_target_pairs={{2,0},{4,2},{6,4},{8,6},{10,8},{12,10},{14,12},{16,14},{18,16},{20... | collective-permute-start | bytes 393224 | tf_op jit(solution)/shard_map/ppermute | solution.py:13
  67.0 7.1 %collective-permute-start.16 = (f32[2,64,256]{2,1,0:T(8,128)S(1)}, f32[2,64,256]{2,1,0:T(8,128)S(1)}, u32[]{:S(2)}, u32[]{:S(2)}) collective-permute-start(f32[2,64,256]{2,1,0:T(8,128)S(1)} %get-tuple-element.17), channel_id=1, source_target_pairs={{0,2},{2,4},{4,6},{6,8},{8,10},{10,12},{12,14},{14,16},{16,18},{18... | collective-permute-start | bytes 393224 | tf_op jit(solution)/shard_map/ppermute | solution.py:13
  74.1 7.9 %collective-permute-start.17 = (f32[2,64,256]{2,1,0:T(8,128)S(1)}, f32[2,64,256]{2,1,0:T(8,128)S(1)}, u32[]{:S(2)}, u32[]{:S(2)}) collective-permute-start(f32[2,64,256]{2,1,0:T(8,128)S(1)} %fusion.28), channel_id=1, source_target_pairs={{0,2},{2,4},{4,6},{6,8},{8,10},{10,12},{12,14},{14,16},{16,18},{18... | collective-permute-start | bytes 393224 | tf_op jit(solution)/shard_map/ppermute | solution.py:13
  78.5 8.0 %collective-permute-start.14 = (f32[2,64,256]{2,1,0:T(8,128)S(1)}, f32[2,64,256]{2,1,0:T(8,128)S(1)}, u32[]{:S(2)}, u32[]{:S(2)}) collective-permute-start(f32[2,64,256]{2,1,0:T(8,128)S(1)} %broadcast_select_fusion.5), channel_id=1, source_target_pairs={{4,0},{6,2},{8,4},{10,6},{12,8},{14,10},{16,12},{18,14},{20,16},{2... | collective-permute-start | bytes 393224 | tf_op jit(solution)/shard_map/ppermute | solution.py:13
  86.6 11.3 %collective-permute-start.15 = (f32[2,64,256]{2,1,0:T(8,128)S(1)}, f32[2,64,256]{2,1,0:T(8,128)S(1)}, u32[]{:S(2)}, u32[]{:S(2)}) collective-permute-start(f32[2,64,256]{2,1,0:T(8,128)S(1)} %broadcast_select_fusion.7), channel_id=1, source_target_pairs={{8,0},{10,2},{12,4},{14,6},{16,8},{18,10},{20,12},{22,14},{24,16},... | collective-permute-start | bytes 393224 | tf_op jit(solution)/shard_map/ppermute | solution.py:13
  89.1 10.8 %collective-permute-start.19 = (f32[2,64,256]{2,1,0:T(8,128)S(1)}, f32[2,64,256]{2,1,0:T(8,128)S(1)}, u32[]{:S(2)}, u32[]{:S(2)}) collective-permute-start(f32[2,64,256]{2,1,0:T(8,128)S(1)} %broadcast_select_fusion.6), channel_id=1, source_target_pairs={{0,8},{2,10},{4,12},{6,14},{8,16},{10,18},{12,20},{14,22},{16,24},... | collective-permute-start | bytes 393224 | tf_op jit(solution)/shard_map/ppermute | solution.py:13
  104.2 7.7 %collective-permute-start.20 = (f32[3,2,64,256]{3,2,1,0:T(8,128)S(1)}, f32[3,2,64,256]{3,2,1,0:T(8,128)S(1)}, u32[]{:S(2)}, u32[]{:S(2)}) collective-permute-start(f32[3,2,64,256]{3,2,1,0:T(8,128)S(1)} %bitcast.145), channel_id=1, source_target_pairs={{1,0},{3,2},{5,4},{7,6},{9,8},{11,10},{13,12},{15,14},{17,16},{19,... | collective-permute-start | bytes 1179656 | tf_op jit(solution)/shard_map/ppermute | solution.py:13
  112.4 7.2 %collective-permute-start.22 = (f32[2,64,256]{2,1,0:T(8,128)S(1)}, f32[2,64,256]{2,1,0:T(8,128)S(1)}, u32[]{:S(2)}, u32[]{:S(2)}) collective-permute-start(f32[2,64,256]{2,1,0:T(8,128)S(1)} %get-tuple-element.14), channel_id=1, source_target_pairs={{2,0},{4,2},{6,4},{8,6},{10,8},{12,10},{14,12},{16,14},{18,16},{20... | collective-permute-start | bytes 393224 | tf_op jit(solution)/shard_map/ppermute | solution.py:13
  115.0 7.1 %collective-permute-start.26 = (f32[2,64,256]{2,1,0:T(8,128)S(1)}, f32[2,64,256]{2,1,0:T(8,128)S(1)}, u32[]{:S(2)}, u32[]{:S(2)}) collective-permute-start(f32[2,64,256]{2,1,0:T(8,128)S(1)} %get-tuple-element.15), channel_id=1, source_target_pairs={{0,2},{2,4},{4,6},{6,8},{8,10},{10,12},{12,14},{14,16},{16,18},{18... | collective-permute-start | bytes 393224 | tf_op jit(solution)/shard_map/ppermute | solution.py:13
  122.2 7.9 %collective-permute-start.27 = (f32[2,64,256]{2,1,0:T(8,128)S(1)}, f32[2,64,256]{2,1,0:T(8,128)S(1)}, u32[]{:S(2)}, u32[]{:S(2)}) collective-permute-start(f32[2,64,256]{2,1,0:T(8,128)S(1)} %fusion.26), channel_id=1, source_target_pairs={{0,2},{2,4},{4,6},{6,8},{8,10},{10,12},{12,14},{14,16},{16,18},{18... | collective-permute-start | bytes 393224 | tf_op jit(solution)/shard_map/ppermute | solution.py:13
  126.6 7.9 %collective-permute-start.24 = (f32[2,64,256]{2,1,0:T(8,128)S(1)}, f32[2,64,256]{2,1,0:T(8,128)S(1)}, u32[]{:S(2)}, u32[]{:S(2)}) collective-permute-start(f32[2,64,256]{2,1,0:T(8,128)S(1)} %broadcast_select_fusion.1), channel_id=1, source_target_pairs={{4,0},{6,2},{8,4},{10,6},{12,8},{14,10},{16,12},{18,14},{20,16},{2... | collective-permute-start | bytes 393224 | tf_op jit(solution)/shard_map/ppermute | solution.py:13
  134.5 11.6 %collective-permute-start.25 = (f32[2,64,256]{2,1,0:T(8,128)S(1)}, f32[2,64,256]{2,1,0:T(8,128)S(1)}, u32[]{:S(2)}, u32[]{:S(2)}) collective-permute-start(f32[2,64,256]{2,1,0:T(8,128)S(1)} %broadcast_select_fusion.3), channel_id=1, source_target_pairs={{8,0},{10,2},{12,4},{14,6},{16,8},{18,10},{20,12},{22,14},{24,16},... | collective-permute-start | bytes 393224 | tf_op jit(solution)/shard_map/ppermute | solution.py:13
  137.0 10.9 %collective-permute-start.29 = (f32[2,64,256]{2,1,0:T(8,128)S(1)}, f32[2,64,256]{2,1,0:T(8,128)S(1)}, u32[]{:S(2)}, u32[]{:S(2)}) collective-permute-start(f32[2,64,256]{2,1,0:T(8,128)S(1)} %broadcast_select_fusion.2), channel_id=1, source_target_pairs={{0,8},{2,10},{4,12},{6,14},{8,16},{10,18},{12,20},{14,22},{16,24},... | collective-permute-start | bytes 393224 | tf_op jit(solution)/shard_map/ppermute | solution.py:13
  (11 other events, 187.0 us)
where the time goes:
time: 153 us; the launch traced here: 152 us
  starting transfers between devices  95.6 us (62%)
  waiting for transfers between devices  18.3 us (12%)
  between operations  16 us (10%)
  local copies, waits for them, and re-layouts  8.59 us (6%)
  other arithmetic  7.91 us (5%)
  matrix products  5.16 us (3%)
    ppermute x30, starting transfers between devices, from_behind(): lax.ppermute(value, axis, [(source, source + steps) for source in range(l...  95.6 us
    ppermute x30, waiting for transfers between devices, from_behind(): lax.ppermute(value, axis, [(source, source + steps) for source in range(l...  18.3 us
    dot_general x3, matrix products, tap_sums(): jnp.einsum('cjzxy,jcab->abzxy', zstack, kernel, precision=lax.Precision.H...  5.16 us
    convert_element_type x1, other arithmetic, body(): return output.astype(jnp.bfloat16)  3.73 us
  transfers between devices with their start and end apart: 30, of which 12 were waited for; matrix products, arithmetic and copies ran while one was open for 2% of the time, Pallas kernels for 0%

commit v1 on v0

v1 whole, which is shorter than its diff:
```python
import functools

import jax
import jax.numpy as jnp
from jax import lax
from jax.experimental import pallas as pl
from jax.experimental.pallas import tpu as pltpu
from jax.sharding import PartitionSpec as P

DMAX = 256
ROWS = 32
CHUNK = 16
SMEM = pl.BlockSpec(memory_space=pltpu.SMEM)
VMEM = pl.BlockSpec(memory_space=pltpu.VMEM)


def pair_gather(value):
    count = lax.axis_size("gy")
    groups = None if count == 2 else [[i, i + 1] for i in range(0, count, 2)]
    return lax.all_gather(value, "gy", axis=0, axis_index_groups=groups)


def widen(field):
    count = lax.axis_size("gy")
    if count == 2:
        return field
    height = field.shape[-1] // 2
    before = lax.ppermute(field[..., height:], "gy", [(i, i + 2) for i in range(count - 2)])
    after = lax.ppermute(field[..., :height], "gy", [(i + 2, i) for i in range(count - 2)])
    return jnp.concatenate([before, field, after], axis=-1)


def outward(value, steps):
    blocks, columns = lax.axis_size("gx"), lax.axis_size("gy")
    moves = []
    for k in range(blocks):
        for g in range(columns):
            target = k - steps if g % 2 == 0 else k + steps
            if 0 <= target < blocks:
                moves.append((k * columns + g, target * columns + g))
    return lax.ppermute(value, ("gx", "gy"), moves)


def branch_counts(width):
    most = -(-DMAX // width)
    parts = width // CHUNK
    return most, parts, most * parts + most


def routes(dilations, width):
    most, parts, total = branch_counts(width)
    bits = total.bit_length()
    route = jnp.where(
        lax.rem(dilations, width) == 0,
        most * parts - 1 + lax.div(dilations, width),
        lax.div(dilations - 1, CHUNK),
    )
    layers = dilations.shape[0]
    packed = jnp.sum(route << (bits * jnp.arange(layers, dtype=jnp.int32)), dtype=jnp.int32)
    return [(packed >> (bits * layer)) & ((1 << bits) - 1) for layer in range(layers)]


def exchange(sent, beside, route):
    width = sent.shape[1]
    most, parts, _ = branch_counts(width)

    def straddling(blocks, part, sent, others):
        near = sent[:, : width - part * CHUNK]
        if blocks > 0:
            near = outward(near, blocks)
        far = outward(sent[:, width - (part + 1) * CHUNK :], blocks + 1)
        made = beside[0](*others)
        return pair_gather(jnp.concatenate([near, far], axis=1)), made

    def exact(blocks, sent, others):
        near = outward(sent, blocks)
        made = beside[0](*others)
        return pair_gather(jnp.concatenate([near, jnp.zeros_like(near[:, :CHUNK])], axis=1)), made

    branches = [
        functools.partial(straddling, blocks, part) for blocks in range(most) for part in range(parts)
    ]
    branches += [functools.partial(exact, blocks) for blocks in range(1, most + 1)]
    return lax.switch(route, branches, sent, beside[1])


def tap_rows(layer, a, maps, weights, reach, rows, halo):
    depth, _, wide = maps[0].shape
    inner = wide - 2 * halo
    loaded = [[ref[z, rows, :].astype(jnp.float32) for z in range(depth)] for ref in maps]
    column = lax.broadcasted_iota(jnp.int32, (loaded[0][0].shape[0], inner), 1)
    sums = []
    for z in range(depth):
        total = None
        for b in (-1, 0, 1):
            part = None
            for j, planes in enumerate(loaded):
                for c in (-1, 0, 1):
                    if 0 <= z + c < depth:
                        weight = weights[layer, j, 9 * (c + 1) + 3 * (a + 1) + (b + 1)]
                        term = weight * planes[z + c]
                        part = term if part is None else part + term
            if b == 1:
                part = pltpu.roll(part, wide - reach, 1)
            elif b == -1:
                part = pltpu.roll(part, reach, 1)
            part = part[:, halo : halo + inner]
            if halo == 0 and b == 1:
                part = jnp.where(column < inner - reach, part, 0.0)
            elif halo == 0 and b == -1:
                part = jnp.where(column >= reach, part, 0.0)
            total = part if total is None else total + part
        sums.append(total)
    return sums


def sent_body(layer, maps, weights, dilations, sent, halo):
    depth, width, _ = sent.shape
    reach = dilations[layer]
    side = lax.rem(lax.axis_index("gy"), 2)

    @pl.loop(0, width, step=ROWS)
    def _(first):
        rows = pl.ds(pl.multiple_of(first, ROWS), ROWS)
        for z, plane in enumerate(tap_rows(layer, 1 - 2 * side, maps, weights, reach, rows, halo)):
            sent[z, rows, :] = plane

    @pl.when(side == 0)
    def _():
        turn = lax.rem(width - lax.rem(reach, width), width)
        for z in range(depth):
            sent[z] = pltpu.roll(sent[z], turn, 0)


def map_body(layer, came, centre, dilations, biases, made):
    depth, width, _ = centre.shape
    turn = lax.rem(dilations[layer], width)
    row = lax.broadcasted_iota(jnp.int32, centre.shape[1:], 0)
    for z in range(depth):
        upper, lower = (
            jnp.where(row < width - turn, came[side, z, :width], came[side, z, CHUNK:]) for side in (0, 1)
        )
        total = centre[z] + upper + pltpu.roll(lower, turn, 0) + biases[layer]
        made[z] = jnp.maximum(total, 0.0).astype(jnp.bfloat16).astype(jnp.float32)


def own_half(ref_shape, write):
    half = ref_shape[-1]
    side = lax.rem(lax.axis_index("gy"), 2)
    for member in (0, 1):
        pl.when(side == member)(functools.partial(write, slice(member * half, (member + 1) * half)))


def first_kernel(dilations, weights, came, made, sent):
    height = came.shape[-1]
    made[:, :, :height] = came[0]
    made[:, :, height:] = came[1]
    sent_body(0, [made], weights, dilations, sent, 0)


def sent_kernel(layer, halo, dilations, weights, *refs):
    sent_body(layer, refs[:-1], weights, dilations, refs[-1], halo)


def map_kernel(layer, dilations, biases, came, centre, made):
    map_body(layer, came, centre, dilations, biases, made)


def layer_kernel(layer, dilations, weights, biases, came, centre, *refs):
    maps, (made, sent) = refs[:layer], refs[layer:]
    map_body(layer - 1, came, centre, dilations, biases, made)
    sent_body(layer, [*maps, made], weights, dilations, sent, 0)


def last_kernel(layers, dilations, biases, mix, came, centre, mixed, out, made):
    map_body(layers - 1, came, centre, dilations, biases, made)

    def write(columns):
        out[...] = (mixed[...] + mix[layers] * made[:, :, columns]).astype(jnp.bfloat16)

    own_half(out.shape, write)


def beside_kernel(layer, last, halo, dilations, weights, mix, *refs):
    maps, (centre, kept) = refs[: layer + 1], refs[layer + 1 :]
    _, width, inner = centre.shape
    reach = dilations[layer]

    @pl.loop(0, width, step=ROWS)
    def _(first):
        rows = pl.ds(pl.multiple_of(first, ROWS), ROWS)
        for z, plane in enumerate(tap_rows(layer, 0, maps, weights, reach, rows, halo)):
            centre[z, rows, :] = plane

    if not last:
        kept[...] = maps[-1][...].astype(jnp.bfloat16)
        return

    def write(columns):
        columns = slice(columns.start + halo, columns.stop + halo)
        kept[...] = sum(mix[j] * ref[:, :, columns].astype(jnp.float32) for j, ref in enumerate(maps))

    own_half(kept.shape, write)


def call(kernel, out_shape, scalars, arrays, scratch=(), cost=None):
    return pl.pallas_call(
        kernel,
        out_shape=out_shape,
        in_specs=[SMEM] * len(scalars) + [VMEM] * len(arrays),
        out_specs=jax.tree.map(lambda _: VMEM, out_shape),
        scratch_shapes=list(scratch),
        cost_estimate=cost,
    )(*scalars, *arrays)


def body(noisy, dilations, conv_weights, biases, mix_weights):
    layers = conv_weights.shape[0]
    depth, width, height = noisy.shape
    paired = lax.axis_size("gy") == 2
    halo = 0 if paired else height
    assert height >= DMAX and lax.axis_size("gy") % 2 == 0 and width % ROWS == 0
    field = jax.ShapeDtypeStruct((depth, width, 2 * height), jnp.float32)
    wide = (depth, width, 2 * (height + halo))
    own = jax.ShapeDtypeStruct(noisy.shape, jnp.float32)
    route = routes(dilations, width)
    cost = pl.CostEstimate(flops=72 * depth * width * 2 * height, bytes_accessed=1 << 20, transcendentals=0)

    def beside(layer, newest, older):
        last = layer == layers - 1
        shapes = (field, own if last else jax.ShapeDtypeStruct(wide, jnp.bfloat16))

        def run(dilations, weights, mix, *maps):
            return call(
                functools.partial(beside_kernel, layer, last, halo),
                shapes,
                (dilations, weights, mix),
                maps,
                cost=cost,
            )

        return run, (dilations, conv_weights, mix_weights, *older, newest)

    def send(layer, newest, older):
        return call(
            functools.partial(sent_kernel, layer, halo), field, (dilations, conv_weights), (*older, newest)
        )

    came = pair_gather(noisy.astype(jnp.float32))
    older = []
    if paired:
        newest, sent = call(first_kernel, (field, field), (dilations, conv_weights), (came,))
    else:
        newest = widen(jnp.concatenate([came[0], came[1]], axis=-1))
        sent = send(0, newest, older)
    for layer in range(1, layers):
        came, (centre, kept) = exchange(sent, beside(layer - 1, newest, older), route[layer - 1])
        older.append(kept)
        if paired:
            newest, sent = call(
                functools.partial(layer_kernel, layer),
                (field, field),
                (dilations, conv_weights, biases),
                (came, centre, *older),
            )
        else:
            newest = call(
                functools.partial(map_kernel, layer - 1), field, (dilations, biases), (came, centre)
            )
            newest = widen(newest)
            sent = send(layer, newest, older)
    came, (centre, mixed) = exchange(sent, beside(layers - 1, newest, older), route[layers - 1])
    return call(
        functools.partial(last_kernel, layers),
        jax.ShapeDtypeStruct(noisy.shape, jnp.bfloat16),
        (dilations, biases, mix_weights),
        (came, centre, mixed),
        scratch=[pltpu.VMEM(field.shape, jnp.float32)],
    )


def solution(mesh):
    return jax.shard_map(
        body,
        mesh=mesh,
        in_specs=(P(None, "gx", "gy"), P(), P(), P(), P()),
        out_specs=P(None, "gx", "gy"),
        check_vma=False,
    )
```

time: 153 us -> 53.1 us (0.35)
  starting transfers between devices: 95.6 us -> 6.46 us
  between operations: 16 us -> 2 us
  blocking collectives: 0 us -> 10.5 us
  Pallas kernels: 0 us -> 8.43 us
  local copies, waits for them, and re-layouts: 8.59 us -> 1.38 us
  other arithmetic: 7.91 us -> 2.19 us
  matrix products: 5.16 us -> 0 us
  waiting for transfers between devices: 18.3 us -> 21.6 us
    ppermute x30 -> x5, starting transfers between devices: 95.6 us -> 6.46 us  [outward(): return lax.ppermute(value, ('gx', 'gy'), moves)]
    all_gather x0 -> x4, blocking collectives: none -> 10.5 us  [pair_gather(): return lax.all_gather(value, 'gy', axis=0, axis_index_groups=groups)]
    pallas_call x0 -> x7, Pallas kernels: none -> 8.43 us  [call(): pl.pallas_call(kernel, out_shape=out_shape, in_specs=[SMEM] * len(scalars...]
    dot_general x3 -> x0, matrix products: 5.16 us -> none  [tap_sums(): jnp.einsum('cjzxy,jcab->abzxy', zstack, kernel, precision=lax.Precision.H...]
    slice x15 -> x4, local copies, waits for them, and re-layouts: 5.19 us -> 0.05 us  [the longest x2 0.03 us: straddling(): near = sent[:, :width - part * CHUNK]]
    convert_element_type x3 -> x0, other arithmetic: 5 us -> none  [the longest x1 3.73 us: body(): return output.astype(jnp.bfloat16)]
    ppermute x30 -> x5, waiting for transfers between devices: 18.3 us -> 21.6 us  [outward(): return lax.ppermute(value, ('gx', 'gy'), moves)]
    another operation x13 -> x0, local copies, waits for them, and re-layouts: 3.13 us -> none  [the longest x9 2.74 us: tap_sums(): jnp.stack([padded[:, shift_index:shift_index + depth] for shift_index in...]
  transfers between devices with their start and end apart: 30 -> 5, of which waited for: 12 -> 3; matrix products, arithmetic and copies ran while one was open for 2% -> 0% of each run, Pallas kernels for 0% -> 6%
where the time goes in v1:
time: 53.1 us; the launch traced here: 53 us
  waiting for transfers between devices  21.6 us (41%)
  blocking collectives  10.5 us (20%)
  Pallas kernels  8.43 us (16%)
  starting transfers between devices  6.46 us (12%)
  other arithmetic  2.19 us (4%)
  between operations  2 us (4%)
  local copies, waits for them, and re-layouts  1.38 us (3%)
    ppermute x5, waiting for transfers between devices, outward(): return lax.ppermute(value, ('gx', 'gy'), moves)  21.6 us
    all_gather x4, blocking collectives, pair_gather(): return lax.all_gather(value, 'gy', axis=0, axis_index_groups=groups)  10.5 us
    pallas_call x7, Pallas kernels, call(): pl.pallas_call(kernel, out_shape=out_shape, in_specs=[SMEM] * len(scalars...  8.43 us
    ppermute x5, starting transfers between devices, outward(): return lax.ppermute(value, ('gx', 'gy'), moves)  6.46 us
    unnamed x6, local copies, waits for them, and re-layouts  1.31 us
    reduce_sum x1, other arithmetic, routes(): jnp.sum(route << bits * jnp.arange(layers, dtype=jnp.int32), dtype=jnp.in...  1.3 us
  transfers between devices with their start and end apart: 5, of which 3 were waited for; matrix products, arithmetic and copies ran while one was open for 0% of the time, Pallas kernels for 6%

profile of v1, /device:TPU:0, one launch (start us, length us, event | category | flops | bytes accessed | tf_op | source)
XLA Modules:
  0.0 53.0 jit_solution(15779955496839702104)
XLA Ops:
  0.0 1.3 %shift-left_reduce_fusion = s32[]{:T(128)} fusion(s32[3]{0:T(128)} %dilations.7), kind=kLoop, calls=%fused_computation.55 | loop fusion | flops 65 | bytes 16 | tf_op jit(solution)/shard_map/reduce_sum | solution.py:59
  3.2 0.9 %all_gather.372 = f32[2,64,256]{2,1,0:T(8,128)S(1)} convert(bf16[2,64,256]{2,1,0:T(8,128)(2,1)} %param.65) | non-fusion elementwise | flops 32768 | bytes 196608 | tf_op jit(solution)/shard_map/all_gather | solution.py:20
  4.1 2.2 %all-gather.60 = f32[4,64,256]{2,1,0:T(8,128)} all-gather(f32[2,64,256]{2,1,0:T(8,128)S(1)} %all_gather.372), channel_id=62, replica_groups=mesh['gx'=16,'gy'=2] {'gy'}, dimensions={0}, use_global_device_ids=true | all-gather | bytes 393216 | tf_op jit(solution)/shard_map/all_gather | solution.py:20
  7.0 1.3 %shard_map.55 = (f32[2,64,512]{2,1,0:T(8,128)S(1)}, f32[2,64,512]{2,1,0:T(8,128)S(1)}) custom-call(s32[3]{0:T(128)S(1)} %copy-done.1, f32[3,4,27]{2,1,0:T(4,128)S(1)} %copy-done, f32[2,2,64,256]{3,2,1,0:T(8,128)} %bitcast.121), custom_call_target="tpu_custom_call" | custom-call | tf_op jit(solution)/shard_map/pallas_call | solution.py:207
  9.0 14.0 %conditional.3 = (f32[2,2,80,512]{3,2,1,0:T(8,128)S(1)}, f32[2,64,512]{2,1,0:T(8,128)S(1)}, bf16[2,64,512]{2,1,0:T(8,128)(2,1)S(1)}) conditional(s32[]{:T(128)} %clamp.11, (f32[2,64,512]{2,1,0:T(8,128)S(1)}, s32[3]{0:T(128)S(1)}, f32[3,4,27]{2,1,0:T(4,128)S(1)}, f32[4]{0:T(128)S(1)}, ...), branch_computations={%region_1.2_spmd, %region_2.3_spmd, %region_3.4_spmd, %region_4.5_... | conditional | flops 4800512 | bytes 4653160 | solution.py:84
  9.0 1.3 %collective-permute-start.18 = (f32[2,48,512]{2,1,0:T(8,128)S(1)}, f32[2,48,512]{2,1,0:T(8,128)S(1)}, u32[]{:S(2)}, u32[]{:S(2)}) collective-permute-start(f32[2,48,512]{2,1,0:T(8,128)S(1)} %slice.151), channel_id=1, source_target_pairs={{1,3},{2,0},{3,5},{4,2},{5,7},{6,4},{7,9},{8,6},{9,11},{10,8},{11,... | collective-permute-start | bytes 589832 | tf_op jit(solution)/shard_map/cond/branch_5_fun/ppermute | solution.py:41
  10.3 1.3 %collective-permute-start.19 = (f32[2,32,512]{2,1,0:T(8,128)S(1)}, f32[2,32,512]{2,1,0:T(8,128)S(1)}, u32[]{:S(2)}, u32[]{:S(2)}) collective-permute-start(f32[2,32,512]{2,1,0:T(8,128)S(1)} %slice.152), channel_id=1, source_target_pairs={{1,5},{3,7},{4,0},{5,9},{6,2},{7,11},{8,4},{9,13},{10,6},{11,15},{... | collective-permute-start | bytes 393224 | tf_op jit(solution)/shard_map/cond/branch_5_fun/ppermute | solution.py:41
  11.6 1.0 %branch_5_fun.3 = (f32[2,64,512]{2,1,0:T(8,128)S(1)}, bf16[2,64,512]{2,1,0:T(8,128)(2,1)S(1)}) custom-call(s32[3]{0:T(128)S(1)} %get-tuple-element.761.dilations, f32[3,4,27]{2,1,0:T(4,128)S(1)} %get-tuple-element.762.weights, f32[4]{0:T(128)S(1)} %get-tuple-element.763.mix, f32[2,64,512]{2,1,0:T(8,128)S(1)} %get-tuple-element.764.refs_0_), custom_call_target="tpu_custom_call" | custom-call | flops 4718592 | bytes 1048576 | tf_op jit(solution)/shard_map/cond/branch_5_fun/pallas_call | solution.py:207
  12.6 7.5 %collective-permute-done.19 = f32[2,32,512]{2,1,0:T(8,128)S(1)} collective-permute-done((f32[2,32,512]{2,1,0:T(8,128)S(1)}, f32[2,32,512]{2,1,0:T(8,128)S(1)}, u32[]{:S(2)}, u32[]{:S(2)}) %collective-permute-start.19) | collective-permute-done | bytes 131104 | tf_op jit(solution)/shard_map/cond/branch_5_fun/ppermute | solution.py:41
  20.1 2.8 %all-gather.5 = f32[4,80,512]{2,1,0:T(8,128)S(1)} all-gather(f32[2,80,512]{2,1,0:T(8,128)S(1)} %pad_maximum_fusion.5), channel_id=7, replica_groups=mesh['gx'=16,'gy'=2] {'gy'}, dimensions={0}, use_global_device_ids=true | all-gather | bytes 983040 | tf_op jit(solution)/shard_map/cond/branch_5_fun/all_gather | solution.py:20
  23.0 1.3 %shard_map.56 = (f32[2,64,512]{2,1,0:T(8,128)S(1)}, f32[2,64,512]{2,1,0:T(8,128)S(1)}) custom-call(s32[3]{0:T(128)S(1)} %copy-done.1, f32[3,4,27]{2,1,0:T(4,128)S(1)} %copy-done, f32[3]{0:T(128)} %biases.5, f32[2,2,80,512]{3,2,1,0:T(8,128)S(1)} %get-tuple-element.1222.came, f32[2,64,512]{2,1,0:T(8,128)S(1)} %get-tuple-element.1223.centre, ...), custom_call_target="tpu_custom_call" | custom-call | tf_op jit(solution)/shard_map/pallas_call | solution.py:207
  24.2 13.7 %conditional.4 = (f32[2,2,80,512]{3,2,1,0:T(8,128)S(1)}, f32[2,64,512]{2,1,0:T(8,128)S(1)}, bf16[2,64,512]{2,1,0:T(8,128)(2,1)S(1)}) conditional(s32[]{:T(128)} %clamp.10, (f32[2,64,512]{2,1,0:T(8,128)S(1)}, s32[3]{0:T(128)S(1)}, f32[3,4,27]{2,1,0:T(4,128)S(1)}, f32[4]{0:T(128)S(1)}, ...), branch_computations={%region_21.22_spmd, %region_22.23_spmd, %region_23.24_spmd, %regio... | conditional | flops 4800512 | bytes 4653160 | solution.py:84
  24.3 1.3 %collective-permute-start.46 = (f32[2,48,512]{2,1,0:T(8,128)S(1)}, f32[2,48,512]{2,1,0:T(8,128)S(1)}, u32[]{:S(2)}, u32[]{:S(2)}) collective-permute-start(f32[2,48,512]{2,1,0:T(8,128)S(1)} %slice.175), channel_id=1, source_target_pairs={{1,3},{2,0},{3,5},{4,2},{5,7},{6,4},{7,9},{8,6},{9,11},{10,8},{11,... | collective-permute-start | bytes 589832 | tf_op jit(solution)/shard_map/cond/branch_5_fun/ppermute | solution.py:41
  25.6 1.3 %collective-permute-start.47 = (f32[2,32,512]{2,1,0:T(8,128)S(1)}, f32[2,32,512]{2,1,0:T(8,128)S(1)}, u32[]{:S(2)}, u32[]{:S(2)}) collective-permute-start(f32[2,32,512]{2,1,0:T(8,128)S(1)} %slice.176), channel_id=1, source_target_pairs={{1,5},{3,7},{4,0},{5,9},{6,2},{7,11},{8,4},{9,13},{10,6},{11,15},{... | collective-permute-start | bytes 393224 | tf_op jit(solution)/shard_map/cond/branch_5_fun/ppermute | solution.py:41
  26.9 1.0 %branch_5_fun.4 = (f32[2,64,512]{2,1,0:T(8,128)S(1)}, bf16[2,64,512]{2,1,0:T(8,128)(2,1)S(1)}) custom-call(s32[3]{0:T(128)S(1)} %get-tuple-element.906.dilations, f32[3,4,27]{2,1,0:T(4,128)S(1)} %get-tuple-element.907.weights, f32[4]{0:T(128)S(1)} %get-tuple-element.908.mix, bf16[2,64,512]{2,1,0:T(8,128)(2,1)S(1)} %get-tuple-element.909.refs_0_, ...), custom_call_target="tpu_custom_call" | custom-call | flops 4718592 | bytes 1048576 | tf_op jit(solution)/shard_map/cond/branch_5_fun/pallas_call | solution.py:207
  27.9 6.8 %collective-permute-done.47 = f32[2,32,512]{2,1,0:T(8,128)S(1)} collective-permute-done((f32[2,32,512]{2,1,0:T(8,128)S(1)}, f32[2,32,512]{2,1,0:T(8,128)S(1)}, u32[]{:S(2)}, u32[]{:S(2)}) %collective-permute-start.47) | collective-permute-done | bytes 131104 | tf_op jit(solution)/shard_map/cond/branch_5_fun/ppermute | solution.py:41
  34.7 3.2 %all-gather.25 = f32[4,80,512]{2,1,0:T(8,128)S(1)} all-gather(f32[2,80,512]{2,1,0:T(8,128)S(1)} %pad_maximum_fusion.21), channel_id=27, replica_groups=mesh['gx'=16,'gy'=2] {'gy'}, dimensions={0}, use_global_device_ids=true | all-gather | bytes 983040 | tf_op jit(solution)/shard_map/cond/branch_5_fun/all_gather | solution.py:20
  37.9 1.4 %shard_map.57 = (f32[2,64,512]{2,1,0:T(8,128)S(1)}, f32[2,64,512]{2,1,0:T(8,128)S(1)}) custom-call(s32[3]{0:T(128)S(1)} %copy-done.1, f32[3,4,27]{2,1,0:T(4,128)S(1)} %copy-done, f32[3]{0:T(128)} %biases.5, f32[2,2,80,512]{3,2,1,0:T(8,128)S(1)} %get-tuple-element.1227.came, f32[2,64,512]{2,1,0:T(8,128)S(1)} %get-tuple-element.1228.centre, ...), custom_call_target="tpu_custom_call" | custom-call | tf_op jit(solution)/shard_map/pallas_call | solution.py:207
  39.3 12.3 %conditional.5 = (f32[2,2,80,512]{3,2,1,0:T(8,128)S(1)}, f32[2,64,512]{2,1,0:T(8,128)S(1)}, f32[2,64,256]{2,1,0:T(8,128)S(1)}) conditional(s32[]{:T(128)} %clamp.9, (f32[2,64,512]{2,1,0:T(8,128)S(1)}, s32[3]{0:T(128)S(1)}, f32[3,4,27]{2,1,0:T(4,128)S(1)}, f32[4]{0:T(128)S(1)}, bf16[2,64,512]{2,1,0:T(8,128)(2,1)S(1)}, ...), branch_computations={%region_41.42_spmd, %region_42.43_spmd, %region_43.44_spmd, %regio... | conditional | flops 4800512 | bytes 4653160 | solution.py:84
  39.6 1.3 %collective-permute-start.11 = (f32[2,64,512]{2,1,0:T(8,128)S(1)}, f32[2,64,512]{2,1,0:T(8,128)S(1)}, u32[]{:S(2)}, u32[]{:S(2)}) collective-permute-start(f32[2,64,512]{2,1,0:T(8,128)S(1)} %get-tuple-element.1196), channel_id=1, source_target_pairs={{1,9},{3,11},{5,13},{7,15},{8,0},{9,17},{10,2},{11,19},{12,4},{13,... | collective-permute-start | bytes 786440 | tf_op jit(solution)/shard_map/cond/branch_19_fun/ppermute | solution.py:41
  40.9 1.1 %branch_19_fun.5 = (f32[2,64,512]{2,1,0:T(8,128)S(1)}, f32[2,64,256]{2,1,0:T(8,128)S(1)}) custom-call(s32[3]{0:T(128)S(1)} %get-tuple-element.1197.dilations, f32[3,4,27]{2,1,0:T(4,128)S(1)} %get-tuple-element.1198.weights, f32[4]{0:T(128)S(1)} %get-tuple-element.1199.mix, bf16[2,64,512]{2,1,0:T(8,128)(2,1)S(1)} %get-tuple-element.1200.refs_0_, ...), custom_call_target="tpu_custom_call" | custom-call | flops 4718592 | bytes 1048576 | tf_op jit(solution)/shard_map/cond/branch_19_fun/pallas_call | solution.py:207
  42.0 7.3 %collective-permute-done.11 = f32[2,64,512]{2,1,0:T(8,128)S(1)} collective-permute-done((f32[2,64,512]{2,1,0:T(8,128)S(1)}, f32[2,64,512]{2,1,0:T(8,128)S(1)}, u32[]{:S(2)}, u32[]{:S(2)}) %collective-permute-start.11) | collective-permute-done | bytes 262176 | tf_op jit(solution)/shard_map/cond/branch_19_fun/ppermute | solution.py:41
  49.3 2.3 %all-gather.59 = f32[4,80,512]{2,1,0:T(8,128)S(1)} all-gather(f32[2,80,512]{2,1,0:T(8,128)S(1)} %concatenate.179), channel_id=61, replica_groups=mesh['gx'=16,'gy'=2] {'gy'}, dimensions={0}, use_global_device_ids=true | all-gather | bytes 983040 | tf_op jit(solution)/shard_map/cond/branch_19_fun/all_gather | solution.py:20
  51.6 1.4 %shard_map.58 = bf16[2,64,256]{2,1,0:T(8,128)(2,1)} custom-call(s32[3]{0:T(128)S(1)} %copy-done.1, f32[3]{0:T(128)} %biases.5, f32[4]{0:T(128)S(1)} %copy-done.2, f32[2,2,80,512]{3,2,1,0:T(8,128)S(1)} %get-tuple-element.1232.came, f32[2,64,512]{2,1,0:T(8,128)S(1)} %get-tuple-element.1233.centre, f32[2,64,256]{2,1,0:T(8,128)S(1)} %get-tuple-element.1234.mixed), custom_call_target="tpu_custom_call" | custom-call | tf_op jit(solution)/shard_map/pallas_call | solution.py:207
  (15 shorter events, 1.4 us)
Async XLA Ops:
  4.1 2.2 %copy-start = (f32[3,4,27]{2,1,0:T(4,128)S(1)}, f32[3,4,27]{2,1,0:T(4,128)}, u32[]{:S(2)}) copy-start(f32[3,4,27]{2,1,0:T(4,128)} %weights.5) | copy-start | bytes 3892
  6.3 0.7 %copy-start.1 = (s32[3]{0:T(128)S(1)}, s32[3]{0:T(128)}, u32[]{:S(2)}) copy-start(s32[3]{0:T(128)} %dilations.7) | copy-start | bytes 40
  8.3 0.7 %copy-start.2 = (f32[4]{0:T(128)S(1)}, f32[4]{0:T(128)}, u32[]{:S(2)}) copy-start(f32[4]{0:T(128)} %mix.1) | copy-start | bytes 52
  9.0 11.1 %collective-permute-start.18 = (f32[2,48,512]{2,1,0:T(8,128)S(1)}, f32[2,48,512]{2,1,0:T(8,128)S(1)}, u32[]{:S(2)}, u32[]{:S(2)}) collective-permute-start(f32[2,48,512]{2,1,0:T(8,128)S(1)} %slice.151), channel_id=1, source_target_pairs={{1,3},{2,0},{3,5},{4,2},{5,7},{6,4},{7,9},{8,6},{9,11},{10,8},{11,... | collective-permute-start | bytes 589832 | tf_op jit(solution)/shard_map/cond/branch_5_fun/ppermute | solution.py:41
  10.3 9.8 %collective-permute-start.19 = (f32[2,32,512]{2,1,0:T(8,128)S(1)}, f32[2,32,512]{2,1,0:T(8,128)S(1)}, u32[]{:S(2)}, u32[]{:S(2)}) collective-permute-start(f32[2,32,512]{2,1,0:T(8,128)S(1)} %slice.152), channel_id=1, source_target_pairs={{1,5},{3,7},{4,0},{5,9},{6,2},{7,11},{8,4},{9,13},{10,6},{11,15},{... | collective-permute-start | bytes 393224 | tf_op jit(solution)/shard_map/cond/branch_5_fun/ppermute | solution.py:41
  24.3 10.4 %collective-permute-start.46 = (f32[2,48,512]{2,1,0:T(8,128)S(1)}, f32[2,48,512]{2,1,0:T(8,128)S(1)}, u32[]{:S(2)}, u32[]{:S(2)}) collective-permute-start(f32[2,48,512]{2,1,0:T(8,128)S(1)} %slice.175), channel_id=1, source_target_pairs={{1,3},{2,0},{3,5},{4,2},{5,7},{6,4},{7,9},{8,6},{9,11},{10,8},{11,... | collective-permute-start | bytes 589832 | tf_op jit(solution)/shard_map/cond/branch_5_fun/ppermute | solution.py:41
  25.6 9.1 %collective-permute-start.47 = (f32[2,32,512]{2,1,0:T(8,128)S(1)}, f32[2,32,512]{2,1,0:T(8,128)S(1)}, u32[]{:S(2)}, u32[]{:S(2)}) collective-permute-start(f32[2,32,512]{2,1,0:T(8,128)S(1)} %slice.176), channel_id=1, source_target_pairs={{1,5},{3,7},{4,0},{5,9},{6,2},{7,11},{8,4},{9,13},{10,6},{11,15},{... | collective-permute-start | bytes 393224 | tf_op jit(solution)/shard_map/cond/branch_5_fun/ppermute | solution.py:41
  39.6 9.7 %collective-permute-start.11 = (f32[2,64,512]{2,1,0:T(8,128)S(1)}, f32[2,64,512]{2,1,0:T(8,128)S(1)}, u32[]{:S(2)}, u32[]{:S(2)}) collective-permute-start(f32[2,64,512]{2,1,0:T(8,128)S(1)} %get-tuple-element.1196), channel_id=1, source_target_pairs={{1,9},{3,11},{5,13},{7,15},{8,0},{9,17},{10,2},{11,19},{12,4},{13,... | collective-permute-start | bytes 786440 | tf_op jit(solution)/shard_map/cond/branch_19_fun/ppermute | solution.py:41
